TPU v7x, 128 devices: a whole 4x4x4 slice. The times are simulated.
128 devices in a mesh: seq: 64 (over y, x, z_lo, core), head: 2 (over z_hi).
Axes of the slice: x: 4, y: 4, z: 4 (z_hi: 2, z_lo: 2; z = z_hi * 2 + z_lo), core: 2. Of those that a mesh axis runs over, the one named last changes fastest.
Arguments:
- queries: bfloat16 [16384, 2048], P(('seq', 'head')), may hold values from -160 to 160
- key_rows: bfloat16 [16384, 2048], P(('seq', 'head')), may hold values from -4 to 4
- value_rows: bfloat16 [16384, 2048], P(('seq', 'head')), may hold values from -6 to 6
- grad_out: bfloat16 [16384, 2048], P(('seq', 'head')), may hold values from -6 to 6
- anchor: int32 [1], replicated, may hold values from 0 to 31
- offsets: int32 [64], replicated, may hold values from 0 to 256
Outputs:
- attended: bfloat16 [16384, 2048], P(('seq', 'head'))
- grad_queries: bfloat16 [16384, 2048], P(('seq', 'head'))
- grad_keys: bfloat16 [16384, 2048], P(('seq', 'head'))
- grad_values: bfloat16 [16384, 2048], P(('seq', 'head'))
All inputs are finite; a program needn't handle non-finite values.
Results may differ from a plain program's by a relative error of at most 0.017.
Values may be sent and summed in bfloat16 or wider, within the bound.
A program may use at most 64 MiB of HBM per device.

v0:
```python
import jax
import jax.numpy as jnp
from jax import lax
from jax.sharding import PartitionSpec as P

DH = 128


def spread(block, axis, owner):
    block = jnp.where(lax.axis_index(axis) == owner, block, jnp.zeros_like(block))
    return lax.psum(block, axis)


def head_scores(query_rows, keys_own, keys_far, visible):
    score_scale = DH ** (-0.5)
    length = query_rows.shape[0]
    query_index = lax.broadcasted_iota(jnp.int32, (length, length), 0)
    key_index = lax.broadcasted_iota(jnp.int32, (length, length), 1)
    score_own = jnp.dot(query_rows, keys_own.T, preferred_element_type=jnp.float32) * score_scale
    score_own = jnp.where(query_index >= key_index, score_own, -jnp.inf)
    score_far = jnp.dot(query_rows, keys_far.T, preferred_element_type=jnp.float32) * score_scale
    score_far = jnp.where(visible[None, :], score_far, -jnp.inf)
    return (score_own, score_far)


def probabilities(score_own, score_far):
    row_max = jnp.maximum(jnp.max(score_own, 1), jnp.max(score_far, 1))
    p_own = jnp.exp(score_own - row_max[:, None])
    p_far = jnp.exp(score_far - row_max[:, None])
    row_total = jnp.sum(p_own, 1) + jnp.sum(p_far, 1)
    return (p_own / row_total[:, None], p_far / row_total[:, None])


def forward_head(query_rows, keys_own, values_own, keys_far, values_far, visible):
    score_own, score_far = head_scores(query_rows, keys_own, keys_far, visible)
    p_own, p_far = probabilities(score_own, score_far)
    w_own = p_own.astype(jnp.bfloat16)
    w_far = p_far.astype(jnp.bfloat16)
    mixed = jnp.dot(w_own, values_own, preferred_element_type=jnp.float32)
    mixed = mixed + jnp.dot(w_far, values_far, preferred_element_type=jnp.float32)
    return (mixed.astype(jnp.bfloat16), p_own, p_far)


def backward_head(
    query_rows, keys_own, values_own, keys_far, values_far, grad_rows, result, p_own, p_far
):
    score_scale = DH ** (-0.5)
    w_own = p_own.astype(jnp.bfloat16)
    w_far = p_far.astype(jnp.bfloat16)
    row_delta = jnp.sum(grad_rows.astype(jnp.float32) * result.astype(jnp.float32), 1)
    d_own = (
        p_own
        * (
            jnp.dot(grad_rows, values_own.T, preferred_element_type=jnp.float32)
            - row_delta[:, None]
        )
    ).astype(jnp.bfloat16)
    d_far = (
        p_far
        * (
            jnp.dot(grad_rows, values_far.T, preferred_element_type=jnp.float32)
            - row_delta[:, None]
        )
    ).astype(jnp.bfloat16)
    grad_q = jnp.dot(d_own, keys_own, preferred_element_type=jnp.float32)
    grad_q = (
        (grad_q + jnp.dot(d_far, keys_far, preferred_element_type=jnp.float32)) * score_scale
    ).astype(jnp.bfloat16)
    own_k = jnp.dot(d_own.T, query_rows, preferred_element_type=jnp.float32) * score_scale
    own_v = jnp.dot(w_own.T, grad_rows, preferred_element_type=jnp.float32)
    far_k = jnp.dot(d_far.T, query_rows, preferred_element_type=jnp.float32) * score_scale
    far_v = jnp.dot(w_far.T, grad_rows, preferred_element_type=jnp.float32)
    return (grad_q, own_k, own_v, far_k, far_v)


def head_slice(x, h):
    return x[:, h * DH : (h + 1) * DH]


def on_device(queries, key_rows, value_rows, grad_out, anchor, offsets):
    q_heads, k_heads, v_heads = (
        lax.all_to_all(queries, "head", split_axis=1, concat_axis=0, tiled=True),
        lax.all_to_all(key_rows, "head", split_axis=1, concat_axis=0, tiled=True),
        lax.all_to_all(value_rows, "head", split_axis=1, concat_axis=0, tiled=True),
    )
    anchor_at = anchor[0]
    stacked = jnp.stack((k_heads, v_heads))
    remote = spread(stacked, "seq", anchor_at)
    k_far = remote[0]
    v_far = remote[1]
    block_index = lax.axis_index("seq")
    length = q_heads.shape[0]
    key_index = jnp.arange(length, dtype=jnp.int32)
    visible_len = lax.dynamic_index_in_dim(offsets, block_index, 0, keepdims=False)
    visible = (block_index > anchor_at) & (key_index < visible_len)
    heads_dev = q_heads.shape[1] // DH
    head_outputs = []
    saved_own = []
    saved_far = []
    for h in range(heads_dev):
        mixed, p_own, p_far = forward_head(
            head_slice(q_heads, h),
            head_slice(k_heads, h),
            head_slice(v_heads, h),
            head_slice(k_far, h),
            head_slice(v_far, h),
            visible,
        )
        head_outputs.append(mixed)
        saved_own.append(p_own)
        saved_far.append(p_far)
    out_heads = jnp.concatenate(head_outputs, 1)
    attended = lax.all_to_all(out_heads, "head", split_axis=0, concat_axis=1, tiled=True)
    g_heads = lax.all_to_all(grad_out, "head", split_axis=1, concat_axis=0, tiled=True)
    parts_q, parts_ko, parts_vo, parts_kf, parts_vf = ([], [], [], [], [])
    for h in range(heads_dev):
        grad_q, own_k, own_v, far_k, far_v = backward_head(
            head_slice(q_heads, h),
            head_slice(k_heads, h),
            head_slice(v_heads, h),
            head_slice(k_far, h),
            head_slice(v_far, h),
            head_slice(g_heads, h),
            head_outputs[h],
            saved_own[h],
            saved_far[h],
        )
        parts_q.append(grad_q)
        parts_ko.append(own_k)
        parts_vo.append(own_v)
        parts_kf.append(far_k)
        parts_vf.append(far_v)
    far_keys = jnp.concatenate(parts_kf, 1)
    far_values = jnp.concatenate(parts_vf, 1)
    summed_k, summed_v = lax.psum((far_keys, far_values), "seq")
    anchor_k = summed_k.astype(jnp.bfloat16)
    anchor_v = summed_v.astype(jnp.bfloat16)
    is_owner = block_index == anchor_at
    grad_k = (
        jnp.concatenate(parts_ko, 1) + jnp.where(is_owner, anchor_k.astype(jnp.float32), 0.0)
    ).astype(jnp.bfloat16)
    grad_v = (
        jnp.concatenate(parts_vo, 1) + jnp.where(is_owner, anchor_v.astype(jnp.float32), 0.0)
    ).astype(jnp.bfloat16)
    grad_q_all = jnp.concatenate(parts_q, 1)
    grad_q_tok, grad_k_tok, grad_v_tok = (
        lax.all_to_all(grad_q_all, "head", split_axis=0, concat_axis=1, tiled=True),
        lax.all_to_all(grad_k, "head", split_axis=0, concat_axis=1, tiled=True),
        lax.all_to_all(grad_v, "head", split_axis=0, concat_axis=1, tiled=True),
    )
    return (attended, grad_q_tok, grad_k_tok, grad_v_tok)


def solution(mesh):
    placed = (
        P(("seq", "head"), None),
        P(("seq", "head"), None),
        P(("seq", "head"), None),
        P(("seq", "head"), None),
        P(),
        P(),
    )
    return jax.shard_map(
        on_device,
        mesh=mesh,
        in_specs=placed,
        out_specs=(
            P(("seq", "head"), None),
            P(("seq", "head"), None),
            P(("seq", "head"), None),
            P(("seq", "head"), None),
        ),
        check_vma=False,
    )
```

profile of v0, /device:TPU:1, one launch (start us, length us, event | category | flops | bytes accessed | tf_op | source)
XLA Modules:
  0.0 1008.5 jit_solution(14595010003698934205)
XLA Ops:
  7.2 2.0 copy.105
  9.2 5.8 all-to-all-start
  15.0 1.0 copy.107
  16.0 7.6 all-to-all-done
  23.6 3.6 all-to-all-start.1
  27.3 1.0 copy.110
  28.9 1.0 copy.122
  32.0 2.8 all-to-all-done.1
  34.9 3.5 all-to-all-start.2
  38.6 0.9 fusion.314
  39.5 0.9 fusion.316
  40.4 0.9 fusion.318
  41.5 3.8 all-to-all-done.2
  45.3 3.5 all-to-all-start.4
  49.0 1.1 maximum_select_fusion
  50.2 0.9 fusion.322
  51.1 0.9 fusion.324
  52.0 0.9 fusion.326
  52.9 0.9 fusion.328
  53.8 1.9 all-to-all-done.4
  55.8 548.3 %all-reduce.4.cloned.1.call-done = bf16[2,256,1024]{2,1,0:T(8,128)(2,1)} async-done(((bf16[2,256,1024]{2,1,0:T(8,128)(2,1)}), bf16[2,256,1024]{2,1,0:T(8,128)(2,1)}) %all-reduce.4.cloned.1.call-update) | async-done | bytes 1048592 | tf_op jit(solution)/shard_map/psum | solution.py:11
  604.1 1.3 slice_bitcast_fusion
  619.4 0.9 fusion.32
  621.1 0.9 fusion.33
  622.8 0.9 fusion.34
  624.6 0.9 fusion.35
  626.3 0.9 fusion.36
  628.1 0.9 fusion.37
  629.8 0.9 fusion.38
  631.5 0.9 fusion.39
  632.4 0.9 fusion.231
  634.2 0.9 convolution_dynamic-update-slice_fusion.7
  636.8 3.8 all-to-all-start.3
  640.6 1.2 fusion.55
  657.4 1.0 convolution_dynamic-update-slice_fusion.14
  668.6 295.8 %all-reduce.5 = (bf16[256,1024]{0,1:T(8,128)(2,1)S(1)}, bf16[256,1024]{0,1:T(8,128)(2,1)S(1)}) all-reduce(f32[256,1024]{0,1:T(8,128)} %copy-done.2, f32[256,1024]{0,1:T(8,128)} %copy-done.4), channel_id=1, replica_groups=mesh['seq'=64,'head'=2] {'seq'}, use_global_device_ids=true, to_apply=%region_41.42 | all-reduce | flops 524288 | bytes 3145728 | tf_op jit(solution)/shard_map/psum | solution.py:135
  965.3 1.9 copy_bitcast_fusion.3
  967.3 4.5 all-to-all-start.5
  971.8 1.8 fusion.96
  974.4 4.3 all-to-all-done.5
  978.7 3.5 all-to-all-start.6
  983.0 6.1 all-to-all-done.6
  989.1 3.5 all-to-all-start.7
  992.6 1.0 copy.143
  993.6 1.0 copy.144
  994.6 1.0 copy.145
  995.6 5.0 all-to-all-done.7
  1000.6 1.0 copy.146
  (258 shorter events, 52.8 us)
Async XLA Ops:
  9.2 5.8 copy-start.37
  9.2 14.4 %all-to-all-start = ((bf16[128,2,1024]{0,2,1:T(8,128)(2,1)}), bf16[128,2,1024]{0,2,1:T(8,128)(2,1)S(1)}, u32[]{:S(2)}, u32[]{:S(2)}) async-start(bf16[128,2,1024]{0,2,1:T(8,128)(2,1)} %bitcast), calls=%async_computation | async-start | bytes 1048576 | tf_op jit(solution)/shard_map/all_to_all | solution.py:82
  23.6 3.6 copy-start.38
  23.6 11.3 %all-to-all-start.1 = ((bf16[128,2,1024]{0,2,1:T(8,128)(2,1)}), bf16[128,2,1024]{0,2,1:T(8,128)(2,1)S(1)}, u32[]{:S(2)}, u32[]{:S(2)}) async-start(bf16[128,2,1024]{0,2,1:T(8,128)(2,1)} %bitcast.3), calls=%async_computation.1 | async-start | bytes 1048576 | tf_op jit(solution)/shard_map/all_to_all | solution.py:83
  27.2 1.7 copy-start.39
  34.9 10.4 %all-to-all-start.2 = ((bf16[128,2,1024]{0,2,1:T(8,128)(2,1)}), bf16[128,2,1024]{0,2,1:T(8,128)(2,1)S(1)}, u32[]{:S(2)}, u32[]{:S(2)}) async-start(bf16[128,2,1024]{0,2,1:T(8,128)(2,1)} %bitcast.9), calls=%async_computation.2 | async-start | bytes 1048576 | tf_op jit(solution)/shard_map/all_to_all | solution.py:84
  41.5 569.9 %copy-start.19 = (f32[256,256]{0,1:T(8,128)}, f32[256,256]{0,1:T(8,128)S(1)}, u32[]{:S(2)}) copy-start(f32[256,256]{0,1:T(8,128)S(1)} %get-tuple-element.55) | copy-start | bytes 786436
  45.3 10.4 %all-to-all-start.4 = ((bf16[128,2,1024]{0,2,1:T(8,128)(2,1)}), bf16[128,2,1024]{0,2,1:T(8,128)(2,1)S(1)}, u32[]{:S(2)}, u32[]{:S(2)}) async-start(bf16[128,2,1024]{0,2,1:T(8,128)(2,1)} %bitcast.17), calls=%async_computation.4 | async-start | bytes 1048576 | tf_op jit(solution)/shard_map/all_to_all | solution.py:114
  48.8 555.3 %all-reduce.4.cloned.1.call-start = ((), (), s32[]{:S(2)}) async-start(), calls=%async_computation.8 | async-start | bytes 2097152 | tf_op jit(solution)/shard_map/psum | solution.py:11
  605.9 15.2 %copy-start.17 = (f32[256,256]{0,1:T(8,128)}, f32[256,256]{0,1:T(8,128)S(1)}, u32[]{:S(2)}) copy-start(f32[256,256]{0,1:T(8,128)S(1)} %get-tuple-element.45) | copy-start | bytes 786436
  606.2 16.6 %copy-start.15 = (f32[256,256]{0,1:T(8,128)}, f32[256,256]{0,1:T(8,128)S(1)}, u32[]{:S(2)}) copy-start(f32[256,256]{0,1:T(8,128)S(1)} %get-tuple-element.51) | copy-start | bytes 786436
  606.5 18.1 %copy-start.13 = (f32[256,256]{0,1:T(8,128)}, f32[256,256]{0,1:T(8,128)S(1)}, u32[]{:S(2)}) copy-start(f32[256,256]{0,1:T(8,128)S(1)} %get-tuple-element.57) | copy-start | bytes 786436
  606.7 19.6 %copy-start.11 = (f32[256,256]{0,1:T(8,128)}, f32[256,256]{0,1:T(8,128)S(1)}, u32[]{:S(2)}) copy-start(f32[256,256]{0,1:T(8,128)S(1)} %get-tuple-element.63) | copy-start | bytes 786436
  607.0 21.0 %copy-start.9 = (f32[256,256]{0,1:T(8,128)}, f32[256,256]{0,1:T(8,128)S(1)}, u32[]{:S(2)}) copy-start(f32[256,256]{0,1:T(8,128)S(1)} %get-tuple-element.69) | copy-start | bytes 786436
  607.3 22.5 %copy-start.7 = (f32[256,256]{0,1:T(8,128)}, f32[256,256]{0,1:T(8,128)S(1)}, u32[]{:S(2)}) copy-start(f32[256,256]{0,1:T(8,128)S(1)} %get-tuple-element.75) | copy-start | bytes 786436
  607.3 1.0 copy-start.23
  607.6 23.9 %copy-start.5 = (f32[256,256]{0,1:T(8,128)}, f32[256,256]{0,1:T(8,128)S(1)}, u32[]{:S(2)}) copy-start(f32[256,256]{0,1:T(8,128)S(1)} %get-tuple-element.81) | copy-start | bytes 786436
  609.7 11.4 %copy-start.53 = (f32[256]{0:T(256)}, f32[256]{0:T(256)S(1)}, u32[]{:S(2)}) copy-start(f32[256]{0:T(256)S(1)} %add.123) | copy-start | bytes 3076
  610.9 11.9 %copy-start.55 = (f32[256]{0:T(256)}, f32[256]{0:T(256)S(1)}, u32[]{:S(2)}) copy-start(f32[256]{0:T(256)S(1)} %add.125) | copy-start | bytes 3076
  611.4 13.2 %copy-start.57 = (f32[256]{0:T(256)}, f32[256]{0:T(256)S(1)}, u32[]{:S(2)}) copy-start(f32[256]{0:T(256)S(1)} %add.127) | copy-start | bytes 3076
  612.7 13.7 %copy-start.59 = (f32[256]{0:T(256)}, f32[256]{0:T(256)S(1)}, u32[]{:S(2)}) copy-start(f32[256]{0:T(256)S(1)} %add.129) | copy-start | bytes 3076
  613.0 15.1 %copy-start.47 = (f32[256]{0:T(256)}, f32[256]{0:T(256)S(1)}, u32[]{:S(2)}) copy-start(f32[256]{0:T(256)S(1)} %max.61) | copy-start | bytes 3076
  613.9 14.2 %copy-start.61 = (f32[256]{0:T(256)}, f32[256]{0:T(256)S(1)}, u32[]{:S(2)}) copy-start(f32[256]{0:T(256)S(1)} %add.131) | copy-start | bytes 3076
  614.2 15.6 %copy-start.49 = (f32[256]{0:T(256)}, f32[256]{0:T(256)S(1)}, u32[]{:S(2)}) copy-start(f32[256]{0:T(256)S(1)} %max.62) | copy-start | bytes 3076
  615.1 14.7 %copy-start.63 = (f32[256]{0:T(256)}, f32[256]{0:T(256)S(1)}, u32[]{:S(2)}) copy-start(f32[256]{0:T(256)S(1)} %add.133) | copy-start | bytes 3076
  615.4 16.1 %copy-start.51 = (f32[256]{0:T(256)}, f32[256]{0:T(256)S(1)}, u32[]{:S(2)}) copy-start(f32[256]{0:T(256)S(1)} %max.63) | copy-start | bytes 3076
  616.3 15.2 %copy-start.65 = (f32[256]{0:T(256)}, f32[256]{0:T(256)S(1)}, u32[]{:S(2)}) copy-start(f32[256]{0:T(256)S(1)} %add.135) | copy-start | bytes 3076
  636.8 330.5 %all-to-all-start.3 = ((bf16[2,128,1024]{1,2,0:T(8,128)(2,1)}), bf16[2,128,1024]{1,2,0:T(8,128)(2,1)S(1)}, u32[]{:S(2)}, u32[]{:S(2)}) async-start(bf16[2,128,1024]{1,2,0:T(8,128)(2,1)} %copy_bitcast_fusion.4), calls=%async_computation.3 | async-start | bytes 1048576 | tf_op jit(solution)/shard_map/all_to_all | solution.py:113
  640.6 1.2 copy-start.35
  640.6 1.2 copy-start.36
  642.7 1.1 copy-start.42
  642.7 1.4 copy-start.43
  642.7 1.6 copy-start.44
  642.7 1.8 copy-start.45
  643.6 2.1 copy-start
  648.0 2.9 copy-start.1
  648.0 1.2 copy-start.30
  648.0 1.5 copy-start.31
  648.0 1.7 copy-start.32
  648.0 2.0 copy-start.33
  649.0 1.9 copy-start.3
  651.2 1.4 copy-start.2
  651.2 1.1 copy-start.16
  651.2 1.1 copy-start.56
  657.4 6.1 copy-start.4
  967.3 11.5 %all-to-all-start.5 = ((bf16[2,128,1024]{1,2,0:T(8,128)(2,1)}), bf16[2,128,1024]{1,2,0:T(8,128)(2,1)S(1)}, u32[]{:S(2)}, u32[]{:S(2)}) async-start(bf16[2,128,1024]{1,2,0:T(8,128)(2,1)} %copy_bitcast_fusion.3), calls=%async_computation.5 | async-start | bytes 1048576 | tf_op jit(solution)/shard_map/all_to_all | solution.py:147
  978.7 10.4 %all-to-all-start.6 = ((bf16[2,128,1024]{1,2,0:T(8,128)(2,1)}), bf16[2,128,1024]{1,2,0:T(8,128)(2,1)S(1)}, u32[]{:S(2)}, u32[]{:S(2)}) async-start(bf16[2,128,1024]{1,2,0:T(8,128)(2,1)} %bitcast.103), calls=%async_computation.6 | async-start | bytes 1048576 | tf_op jit(solution)/shard_map/all_to_all | solution.py:148
  989.1 11.5 %all-to-all-start.7 = ((bf16[2,128,1024]{1,2,0:T(8,128)(2,1)}), bf16[2,128,1024]{1,2,0:T(8,128)(2,1)S(1)}, u32[]{:S(2)}, u32[]{:S(2)}) async-start(bf16[2,128,1024]{1,2,0:T(8,128)(2,1)} %bitcast.102), calls=%async_computation.7 | async-start | bytes 1048576 | tf_op jit(solution)/shard_map/all_to_all | solution.py:149
  (29 other events, 26.9 us)
Sparse Core Ops, SparseCore 0:
  52.1 551.9 all-reduce.3
where the time goes:
time: 1020 us; the launch traced here: 1010 us
  waiting for transfers between devices  580 us (57%)
  blocking collectives  296 us (29%)
  matrix products  50 us (5%)
  starting transfers between devices  31.8 us (3%)
  local copies, waits for them, and re-layouts  29.6 us (3%)
  between operations  15.7 us (2%)
    psum x1, waiting for transfers between devices, spread(): return lax.psum(block, axis)  548 us
    psum x1, blocking collectives, on_device(): summed_k, summed_v = lax.psum((far_keys, far_values), 'seq')  296 us
    unnamed x144, local copies, waits for them, and re-layouts  22.7 us
  transfers between devices with their start and end apart: 9, of which 8 were waited for; matrix products, arithmetic and copies ran while one was open for 4% of the time, Pallas kernels for 0%

commit v1 on v0

v1 whole, which is shorter than its diff:
```python
import jax
import jax.numpy as jnp
from jax import lax
from jax.experimental import pallas as pl
from jax.experimental.pallas import tpu as pltpu
from jax.sharding import PartitionSpec as P

DH = 128
BLOCK = 256
HALF = 128
HEADS = 8
WIDE = HEADS * DH
PLANE = 16
SCALE = DH**-0.5
MESH = pl.DeviceIdType.MESH
LOW = -1e30
EARLY = 4


def dot_t(a, b):
    return lax.dot_general(a, b, (((1,), (1,)), ((), ())), preferred_element_type=jnp.float32)


def t_dot(a, b):
    return lax.dot_general(a, b, (((0,), (0,)), ((), ())), preferred_element_type=jnp.float32)


def dot(a, b):
    return jnp.dot(a, b, preferred_element_type=jnp.float32)


def kernel(
    anchor, offsets, q_in, k_in, v_in, g_in,
    att_out, gq_out, gk_out, gv_out,
    qb, gb, kc, vc, sel, cand, zb, kva, fk, rin, zs, zr, an, ank,
    okf, ovf, pk, pr, att_b, gq_b, gk_b, gv_b,
    in_l, in_s, in_r, pv_s, pv_r, s1_s, s1_r, s2_s, s2_r, s3_s, s3_r,
    r1_s, r1_r, r2_s, r2_r, r3_s, r3_r, pg_s, pg_r, out_l, out_s, out_r,
):
    seq = lax.axis_index("seq")
    t = lax.axis_index("head")
    xy = seq // 4
    zl = lax.rem(seq // 2, 2)
    c = lax.rem(seq, 2)
    other = 1 - c
    z = t * 2 + zl
    low_y = xy < 8

    def at(xy_, z_, c_):
        return (xy_ * 4 + lax.rem(z_, 2) * 2 + c_, z_ // 2)

    sibling = at(xy, z, other)
    partner = at(xy, lax.rem(z + 2, 4), c)

    def plane_dev(j):
        return at(j, z, c)

    def z_dev(z_):
        return at(xy, z_, c)

    def remote(src, dst, ss, rs, dev):
        return pltpu.make_async_remote_copy(
            src_ref=src, dst_ref=dst, send_sem=ss, recv_sem=rs, device_id=dev, device_id_type=MESH
        )

    def head_cols(h):
        return pl.ds(pl.multiple_of(h * DH, DH), DH)

    mine = pl.ds(pl.multiple_of(c * WIDE, WIDE), WIDE)
    theirs = pl.ds(pl.multiple_of(other * WIDE, WIDE), WIDE)
    own_rows = pl.ds(HALF, HALF)
    prev_rows = pl.ds(0, HALF)
    all_rows = pl.ds(0, HALF)

    ins = ((k_in, kc, own_rows), (v_in, vc, own_rows), (q_in, qb, all_rows), (g_in, gb, all_rows))
    local_in = [
        pltpu.make_async_copy(src.at[:, mine], buf.at[c, rows, :], in_l.at[i])
        for i, (src, buf, rows) in enumerate(ins)
    ]
    remote_in = [
        remote(src.at[:, theirs], buf.at[c, rows, :], in_s.at[i], in_r.at[i], sibling)
        for i, (src, buf, rows) in enumerate(ins)
    ]
    for copy in local_in:
        copy.start()

    barrier = pltpu.get_barrier_semaphore()
    pl.semaphore_signal(barrier, inc=1, device_id=sibling, device_id_type=MESH)
    for dz in range(1, 4):
        pl.semaphore_signal(barrier, inc=1, device_id=z_dev(lax.rem(z + dz, 4)), device_id_type=MESH)

    @pl.loop(1, PLANE)
    def _(j):
        pl.semaphore_signal(barrier, inc=1, device_id=plane_dev(lax.rem(xy + j, PLANE)), device_id_type=MESH)

    @pl.when(t == 0)
    def _():
        kc[:, 0:HALF, :] = jnp.zeros((2, HALF, WIDE), jnp.bfloat16)
        vc[:, 0:HALF, :] = jnp.zeros((2, HALF, WIDE), jnp.bfloat16)

    pl.semaphore_wait(barrier, 4 + PLANE - 1)

    for copy in remote_in:
        copy.start()

    a = anchor[0]
    a_core = lax.rem(a, 2)
    a_zl = lax.rem(a // 2, 2)
    a_xy = a // 4

    for i in range(2):
        local_in[i].wait()
        remote_in[i].wait_recv()

    for kv, buf in enumerate((kc, vc)):
        for h in range(HEADS):
            cols = slice(h * DH, (h + 1) * DH)
            sel[kv * HEADS + h] = jnp.where(
                a_core == 0, buf[0, HALF:BLOCK, cols], buf[1, HALF:BLOCK, cols]
            )

    def s1_copy(j):
        return remote(sel.at[j], cand.at[lax.rem(xy, 8)], s1_s.at[j], s1_r.at[lax.rem(xy, 8)], plane_dev(j))

    @pl.when(low_y)
    def _():
        @pl.loop(1, PLANE)
        def _(i):
            s1_copy(lax.rem(xy + i, PLANE)).start()

        cand[lax.rem(xy, 8)] = sel[xy]

    def pv_copy(h, i):
        p, buf = i // 2, (kc, vc)[i % 2]
        cols = head_cols(h)
        return remote(
            buf.at[p, own_rows, cols], buf.at[p, prev_rows, cols], pv_s.at[h, i], pv_r.at[h, i], partner
        )

    def send_first_halves(begin, end):
        @pl.when(t == 0)
        def _():
            @pl.loop(begin, end)
            def _(i):
                h = lax.rem(xy + i, HEADS)
                for k in range(4):
                    pv_copy(h, k).start()

    send_first_halves(0, EARLY)

    @pl.loop(0, 8)
    def _(slot):
        @pl.when(slot != xy)
        def _():
            remote(sel.at[0], cand.at[slot], s1_s.at[0], s1_r.at[slot], sibling).wait_recv()

    zb[z] = cand[a_xy]

    def s2_copy(dz):
        return remote(zb.at[z], zb.at[z], s2_s.at[dz], s2_r.at[z], z_dev(lax.rem(z + dz, 4)))

    for dz in range(1, 4):
        s2_copy(dz).start()
    send_first_halves(EARLY, HEADS)
    for dz in range(1, 4):
        slot = lax.rem(z + dz, 4)
        remote(zb.at[slot], zb.at[slot], s2_s.at[dz], s2_r.at[slot], sibling).wait_recv()
    kva[xy, 0:HALF, :] = zb[a_zl]
    kva[xy, HALF:BLOCK, :] = zb[2 + a_zl]

    def s3_copy(j):
        return remote(kva.at[xy], kva.at[xy], s3_s.at[j], s3_r.at[xy], plane_dev(j))

    @pl.loop(0, PLANE - 1)
    def _(i):
        step = i + 1
        j = lax.rem(xy + PLANE - step // 2 + 8 * lax.rem(step, 2), PLANE)
        s3_copy(j).start()

    for i in range(2, 4):
        local_in[i].wait()
        remote_in[i].wait_recv()

    block0 = seq - c
    row = lax.broadcasted_iota(jnp.int32, (HALF, BLOCK), 0)
    col = lax.broadcasted_iota(jnp.int32, (HALF, BLOCK), 1)
    own_ok = jnp.where(col < HALF, jnp.where(t == 1, 1, 0), jnp.where(row >= col - HALF, 1, 0)) > 0
    own_bias = jnp.where(own_ok, 0.0, LOW)
    own_bias = jnp.concatenate([own_bias, own_bias], 0)
    far_bias = jnp.concatenate(
        [
            jnp.where(col < jnp.where(block0 + p > a, offsets[block0 + p], 0), 0.0, LOW)
            for p in range(2)
        ],
        0,
    )

    def r1_copy(j):
        return remote(fk.at[j], rin.at[xy], r1_s.at[j], r1_r.at[xy], plane_dev(j))

    def pg_copy(h):
        return remote(pk.at[h], pr.at[h], pg_s.at[h], pg_r.at[h], partner)

    @pl.loop(0, HEADS)
    def _(i):
        h = lax.rem(xy + i, HEADS)
        cols = head_cols(h)

        for kv in range(2):
            slot = kv * HEADS + h

            @pl.when(slot != xy)
            def _():
                remote(kva.at[slot], kva.at[slot], s3_s.at[0], s3_r.at[slot], sibling).wait_recv()

        @pl.when(t == 1)
        def _():
            for k in range(4):
                pv_copy(h, k).wait_recv()

        q = [qb[p, :, cols] for p in range(2)]
        g = [gb[p, :, cols] for p in range(2)]
        keys = [kc[p, :, cols] for p in range(2)]
        values = [vc[p, :, cols] for p in range(2)]
        q2 = jnp.concatenate(q, 0)
        g2 = jnp.concatenate(g, 0)
        ka = kva[h]
        va = kva[HEADS + h]
        s_far = dot_t(q2, ka) * SCALE + far_bias
        s_own = jnp.concatenate([dot_t(q[p], keys[p]) for p in range(2)], 0) * SCALE + own_bias
        top = jnp.maximum(jnp.max(s_own, 1, keepdims=True), jnp.max(s_far, 1, keepdims=True))
        e_own = jnp.exp(s_own - top)
        e_far = jnp.exp(s_far - top)
        total = jnp.sum(e_own, 1, keepdims=True) + jnp.sum(e_far, 1, keepdims=True)
        inv = 1.0 / total
        p_own = e_own * inv
        p_far = e_far * inv
        w_own = p_own.astype(jnp.bfloat16)
        w_far = p_far.astype(jnp.bfloat16)
        w_half = [w_own[p * HALF : (p + 1) * HALF] for p in range(2)]
        mixed = dot(w_far, va) + jnp.concatenate([dot(w_half[p], values[p]) for p in range(2)], 0)
        att = mixed.astype(jnp.bfloat16)
        delta = jnp.sum(g2.astype(jnp.float32) * att.astype(jnp.float32), 1, keepdims=True)
        d_far = (p_far * (dot_t(g2, va) - delta)).astype(jnp.bfloat16)
        dp_own = jnp.concatenate([dot_t(g[p], values[p]) for p in range(2)], 0)
        d_own = (p_own * (dp_own - delta)).astype(jnp.bfloat16)
        d_half = [d_own[p * HALF : (p + 1) * HALF] for p in range(2)]
        fk[h] = (t_dot(d_far, q2) * SCALE).astype(jnp.bfloat16)
        fk[HEADS + h] = t_dot(w_far, g2).astype(jnp.bfloat16)
        for kv in range(2):
            j = kv * HEADS + h

            @pl.when(j != xy)
            def _():
                r1_copy(j).start()

        for p in range(2):
            own_k = t_dot(d_half[p], q[p]) * SCALE
            own_v = t_dot(w_half[p], g[p])
            pk[h, 0, p] = own_k[:HALF].astype(jnp.bfloat16)
            pk[h, 1, p] = own_v[:HALF].astype(jnp.bfloat16)
            okf[p, :, cols] = own_k[HALF:]
            ovf[p, :, cols] = own_v[HALF:]

        @pl.when(t == 1)
        def _():
            pg_copy(h).start()

        grad_q = dot(d_far, ka) + jnp.concatenate([dot(d_half[p], keys[p]) for p in range(2)], 0)
        grad_q = (grad_q * SCALE).astype(jnp.bfloat16)
        for p in range(2):
            att_b[p, :, cols] = att[p * HALF : (p + 1) * HALF]
            gq_b[p, :, cols] = grad_q[p * HALF : (p + 1) * HALF]

    outs = ((att_b, att_out), (gq_b, gq_out), (gk_b, gk_out), (gv_b, gv_out))
    local_out = [
        pltpu.make_async_copy(buf.at[c], dst.at[:, mine], out_l.at[i]) for i, (buf, dst) in enumerate(outs)
    ]
    remote_out = [
        remote(buf.at[other], dst.at[:, mine], out_s.at[i], out_r.at[i], sibling)
        for i, (buf, dst) in enumerate(outs)
    ]
    for i in range(2):
        remote_out[i].start()
        local_out[i].start()

    @pl.loop(0, PLANE)
    def _(slot):
        @pl.when(slot != xy)
        def _():
            remote(fk.at[slot], rin.at[slot], r1_s.at[0], r1_r.at[slot], sibling).wait_recv()

    rin[xy] = fk[xy]
    acc = rin[0].astype(jnp.float32)
    for slot in range(1, PLANE):
        acc = acc + rin[slot].astype(jnp.float32)
    zs[0] = acc[:HALF].astype(jnp.bfloat16)
    zs[1] = acc[HALF:].astype(jnp.bfloat16)

    def r2_copy(dz):
        z_ = lax.rem(z + dz, 4)
        return remote(zs.at[z_ // 2], zr.at[z], r2_s.at[dz], r2_r.at[z], z_dev(z_))

    for dz in range(1, 4):
        r2_copy(dz).start()
    zr[z] = zs[t]
    for dz in range(1, 4):
        slot = lax.rem(z + dz, 4)
        remote(zs.at[0], zr.at[slot], r2_s.at[dz], r2_r.at[slot], sibling).wait_recv()
    total = zr[0].astype(jnp.float32)
    for slot in range(1, 4):
        total = total + zr[slot].astype(jnp.float32)
    an[...] = total.astype(jnp.bfloat16)

    def r3_copy(j):
        return remote(an, ank.at[xy], r3_s.at[j], r3_r.at[xy], plane_dev(j))

    @pl.loop(0, 8)
    def _(i):
        j = lax.rem(xy + i, 8)

        @pl.when(j != xy)
        def _():
            r3_copy(j).start()

    @pl.when(t == 0)
    def _():
        @pl.loop(0, HEADS)
        def _(i):
            h = lax.rem(xy + i, HEADS)
            pg_copy(h).wait_recv()
            cols = head_cols(h)
            for p in range(2):
                okf[p, :, cols] += pr[h, 0, p].astype(jnp.float32)
                ovf[p, :, cols] += pr[h, 1, p].astype(jnp.float32)

    @pl.when(low_y)
    def _():
        ank[xy] = an[...]

        @pl.loop(0, PLANE)
        def _(slot):
            @pl.when(slot != xy)
            def _():
                remote(an, ank.at[slot], r3_s.at[0], r3_r.at[slot], sibling).wait_recv()

    for p in (other, c):
        for kv, (grads, out) in enumerate(((okf, gk_b), (ovf, gv_b))):
            owner = block0 + p == a

            @pl.when(low_y)
            def _():
                for h in range(HEADS):
                    cols = slice(h * DH, (h + 1) * DH)
                    far = jnp.where(owner, ank[kv * HEADS + h].astype(jnp.float32), 0.0)
                    out[p, :, cols] = (grads[p, :, cols] + far).astype(jnp.bfloat16)

            @pl.when(jnp.logical_not(low_y))
            def _():
                out[p] = grads[p].astype(jnp.bfloat16)

            if p is other:
                remote_out[2 + kv].start()
            else:
                local_out[2 + kv].start()

    for copy in remote_in:
        copy.wait_send()

    @pl.when(low_y)
    def _():
        @pl.loop(1, PLANE)
        def _(i):
            s1_copy(lax.rem(xy + i, PLANE)).wait_send()

    @pl.when(t == 0)
    def _():
        @pl.loop(0, HEADS)
        def _(h):
            for k in range(4):
                pv_copy(h, k).wait_send()

    @pl.when(t == 1)
    def _():
        @pl.loop(0, HEADS)
        def _(h):
            pg_copy(h).wait_send()

    for dz in range(1, 4):
        s2_copy(dz).wait_send()
        r2_copy(dz).wait_send()

    @pl.loop(0, PLANE)
    def _(j):
        @pl.when(j != xy)
        def _():
            s3_copy(j).wait_send()
            r1_copy(j).wait_send()

    @pl.loop(0, 8)
    def _(j):
        @pl.when(j != xy)
        def _():
            r3_copy(j).wait_send()

    for copy in local_out:
        copy.wait()
    for copy in remote_out:
        copy.wait()


def write_out(*refs):
    sems, sems2, hold = refs[8:]
    first = [pltpu.make_async_copy(refs[i], hold.at[i], sems.at[i]) for i in range(4)]
    second = [pltpu.make_async_copy(hold.at[i], refs[4 + i], sems2.at[i]) for i in range(4)]
    for copy in first:
        copy.start()
    for i in range(4):
        first[i].wait()
        second[i].start()
    for copy in second:
        copy.wait()


def on_device(queries, key_rows, value_rows, grad_out, anchor, offsets):
    bf16, f32 = jnp.bfloat16, jnp.float32
    any_spec = pl.BlockSpec(memory_space=pl.ANY)
    smem_spec = pl.BlockSpec(memory_space=pltpu.SMEM)
    dma = pltpu.SemaphoreType.DMA
    half = (HALF, DH)
    whole = (BLOCK, DH)
    scratch = [
        pltpu.VMEM((2, HALF, WIDE), bf16),
        pltpu.VMEM((2, HALF, WIDE), bf16),
        pltpu.VMEM((2, BLOCK, WIDE), bf16),
        pltpu.VMEM((2, BLOCK, WIDE), bf16),
        pltpu.VMEM((PLANE, *half), bf16),
        pltpu.VMEM((8, *half), bf16),
        pltpu.VMEM((4, *half), bf16),
        pltpu.VMEM((PLANE, *whole), bf16),
        pltpu.VMEM((PLANE, *whole), bf16),
        pltpu.VMEM((PLANE, *whole), bf16),
        pltpu.VMEM((2, *half), bf16),
        pltpu.VMEM((4, *half), bf16),
        pltpu.VMEM(half, bf16),
        pltpu.VMEM((PLANE, *half), bf16),
        pltpu.VMEM((2, HALF, WIDE), f32),
        pltpu.VMEM((2, HALF, WIDE), f32),
        pltpu.VMEM((HEADS, 2, 2, *half), bf16),
        pltpu.VMEM((HEADS, 2, 2, *half), bf16),
        pltpu.VMEM((2, HALF, WIDE), bf16),
        pltpu.VMEM((2, HALF, WIDE), bf16),
        pltpu.VMEM((2, HALF, WIDE), bf16),
        pltpu.VMEM((2, HALF, WIDE), bf16),
        dma((4,)), dma((4,)), dma((4,)),
        dma((HEADS, 4)), dma((HEADS, 4)),
        dma((PLANE,)), dma((8,)),
        dma((4,)), dma((4,)),
        dma((PLANE,)), dma((PLANE,)),
        dma((PLANE,)), dma((PLANE,)),
        dma((4,)), dma((4,)),
        dma((8,)), dma((PLANE,)),
        dma((HEADS,)), dma((HEADS,)),
        dma((4,)), dma((4,)), dma((4,)),
    ]
    results = pl.pallas_call(
        kernel,
        out_shape=[jax.ShapeDtypeStruct(queries.shape, bf16)] * 4,
        in_specs=[smem_spec, smem_spec] + [pl.BlockSpec(memory_space=pltpu.HBM)] * 4,
        out_specs=[any_spec] * 4,
        scratch_shapes=scratch,
        compiler_params=pltpu.CompilerParams(
            collective_id=0, has_side_effects=True, vmem_limit_bytes=60 * 2**20
        ),
        name="anchor_attention",
    )(anchor, offsets, queries, key_rows, value_rows, grad_out)
    return pl.pallas_call(
        write_out,
        out_shape=[jax.ShapeDtypeStruct(queries.shape, bf16)] * 4,
        in_specs=[any_spec] * 4,
        out_specs=[pl.BlockSpec(memory_space=pltpu.HBM)] * 4,
        scratch_shapes=[dma((4,)), dma((4,)), pltpu.VMEM((4, *queries.shape), bf16)],
        name="write_out",
    )(*results)


def solution(mesh):
    tokens = P(("seq", "head"), None)
    return jax.shard_map(
        on_device,
        mesh=mesh,
        in_specs=(tokens, tokens, tokens, tokens, P(), P()),
        out_specs=(tokens, tokens, tokens, tokens),
        check_vma=False,
    )
```

time: 1020 us -> 76.6 us (0.08)
  waiting for transfers between devices: 580 us -> 0 us
  blocking collectives: 296 us -> 0 us
  Pallas kernels: 0 us -> 73.9 us
  matrix products: 50 us -> 0 us
  starting transfers between devices: 31.8 us -> 0 us
  local copies, waits for them, and re-layouts: 29.6 us -> 0 us
  between operations: 15.7 us -> 1.29 us
    psum x1 -> x0, waiting for transfers between devices: 548 us -> none  [spread(): return lax.psum(block, axis)]
    psum x1 -> x0, blocking collectives: 296 us -> none  [on_device(): summed_k, summed_v = lax.psum((far_keys, far_values), 'seq')]
    pallas_call x0 -> x2, Pallas kernels: none -> 73.9 us  [the longest x1 71.4 us: on_device(): pl.pallas_call(kernel, out_shape=[jax.ShapeDtypeStruct(queries.shape, bf1...]
    dot_general x96 -> x0, matrix products: 50 us -> none  [the longest x8 7.14 us: backward_head(): jnp.dot(grad_rows, values_far.T, preferred_element_type=jnp.float32)]
    all_to_all x8 -> x0, starting transfers between devices: 31.8 us -> none  [the longest x1 5.82 us: on_device(): lax.all_to_all(queries, 'head', split_axis=1, concat_axis=0, tiled=True)]
    all_to_all x8 -> x0, waiting for transfers between devices: 31.4 us -> none  [the longest x1 7.57 us: on_device(): lax.all_to_all(queries, 'head', split_axis=1, concat_axis=0, tiled=True)]
    unnamed x144 -> x0, local copies, waits for them, and re-layouts: 22.7 us -> none
  transfers between devices with their start and end apart: 9 -> 0, of which waited for: 8 -> 0; matrix products, arithmetic and copies ran while one was open for 4% -> 0% of each run, Pallas kernels for 0% -> 0%
where the time goes in v1:
time: 76.6 us; the launch traced here: 75.2 us
  Pallas kernels  73.9 us (96%)
  between operations  1.29 us (2%)
    pallas_call x1, Pallas kernels, on_device(): pl.pallas_call(kernel, out_shape=[jax.ShapeDtypeStruct(queries.shape, bf1...  71.4 us
    pallas_call x1, Pallas kernels, on_device(): pl.pallas_call(write_out, out_shape=[jax.ShapeDtypeStruct(queries.shape,...  2.42 us

profile of v1, /device:TPU:1, one launch (start us, length us, event | category | flops | bytes accessed | tf_op | source)
XLA Modules:
  0.0 75.2 jit_solution(11702107694939093185)
XLA Ops:
  1.3 71.4 %anchor_attention.1 = (bf16[128,2048]{1,0:T(8,128)(2,1)}, bf16[128,2048]{1,0:T(8,128)(2,1)}, bf16[128,2048]{1,0:T(8,128)(2,1)}, bf16[128,2048]{1,0:T(8,128)(2,1)}) custom-call(s32[1]{0:T(128)S(6)} %copy.10.anchor, s32[64]{0:T(128)} %offsets.1, bf16[128,2048]{1,0:T(8,128)(2,1)} %q_in.1, bf16[128,2048]{1,0:T(8,128)(2,1)} %k_in.1, bf16[128,2048]{1,0:T(8,128)(2,1)} %v_in.1, ...), custom_call_target="tpu_custom_call" | custom-call | tf_op jit(solution)/shard_map/anchor_attention/pallas_call | solution.py:466
  72.7 2.4 %write_out.1 = (bf16[128,2048]{1,0:T(8,128)(2,1)}, bf16[128,2048]{1,0:T(8,128)(2,1)}, bf16[128,2048]{1,0:T(8,128)(2,1)}, bf16[128,2048]{1,0:T(8,128)(2,1)}) custom-call(bf16[128,2048]{1,0:T(8,128)(2,1)} %get-tuple-element.8.refs_0_, bf16[128,2048]{1,0:T(8,128)(2,1)} %get-tuple-element.9.refs_1_, bf16[128,2048]{1,0:T(8,128)(2,1)} %get-tuple-element.10.refs_2_, ...), custom_call_target="tpu_custom_call" | custom-call | tf_op jit(solution)/shard_map/write_out/pallas_call | solution.py:477

commit v2 on v1

--- a/solution.py
+++ b/solution.py
@@ -14,7 +14,8 @@
 SCALE = DH**-0.5
 MESH = pl.DeviceIdType.MESH
 LOW = -1e30
-EARLY = 4
+EARLY = 3
+EARLY_BACK = 3
 
 
 def dot_t(a, b):
@@ -33,9 +34,9 @@
     anchor, offsets, q_in, k_in, v_in, g_in,
     att_out, gq_out, gk_out, gv_out,
     qb, gb, kc, vc, sel, cand, zb, kva, fk, rin, zs, zr, an, ank,
-    okf, ovf, pk, pr, att_b, gq_b, gk_b, gv_b,
-    in_l, in_s, in_r, pv_s, pv_r, s1_s, s1_r, s2_s, s2_r, s3_s, s3_r,
-    r1_s, r1_r, r2_s, r2_r, r3_s, r3_r, pg_s, pg_r, out_l, out_s, out_r,
+    okf, ovf, q1b, g1b, st, sr, att_b, gq_b, gk_b, gv_b,
+    in_l, in_s, in_r, sw_s, sw_r, s1_s, s1_r, s2_s, s2_r, s3_s, s3_r,
+    r1_s, r1_r, r2_s, r2_r, r3_s, r3_r, st_s, st_r, out_l, out_s, out_r,
 ):
     seq = lax.axis_index("seq")
     t = lax.axis_index("head")
@@ -98,6 +99,7 @@
         kc[:, 0:HALF, :] = jnp.zeros((2, HALF, WIDE), jnp.bfloat16)
         vc[:, 0:HALF, :] = jnp.zeros((2, HALF, WIDE), jnp.bfloat16)
 
+    st[...] = jnp.zeros_like(st)
     pl.semaphore_wait(barrier, 4 + PLANE - 1)
 
     for copy in remote_in:
@@ -130,23 +132,31 @@
 
         cand[lax.rem(xy, 8)] = sel[xy]
 
-    def pv_copy(h, i):
-        p, buf = i // 2, (kc, vc)[i % 2]
+    def swap_copy(h, i, back):
+        p = i // 2
         cols = head_cols(h)
+        if back:
+            buf, far_buf, rows, far_rows = (qb, gb)[i % 2], (q1b, g1b)[i % 2], all_rows, all_rows
+        else:
+            buf, far_buf, rows, far_rows = (kc, vc)[i % 2], (kc, vc)[i % 2], own_rows, prev_rows
         return remote(
-            buf.at[p, own_rows, cols], buf.at[p, prev_rows, cols], pv_s.at[h, i], pv_r.at[h, i], partner
+            buf.at[p, rows, cols], far_buf.at[p, far_rows, cols], sw_s.at[h, i], sw_r.at[h, i], partner
         )
 
-    def send_first_halves(begin, end):
-        @pl.when(t == 0)
+    def swap(begin, end, back):
+        @pl.when(t == (1 if back else 0))
         def _():
             @pl.loop(begin, end)
             def _(i):
                 h = lax.rem(xy + i, HEADS)
                 for k in range(4):
-                    pv_copy(h, k).start()
-
-    send_first_halves(0, EARLY)
+                    swap_copy(h, k, back).start()
+
+    swap(0, EARLY, False)
+    for i in range(2, 4):
+        local_in[i].wait()
+        remote_in[i].wait_recv()
+    swap(0, EARLY_BACK, True)
 
     @pl.loop(0, 8)
     def _(slot):
@@ -161,7 +171,6 @@
 
     for dz in range(1, 4):
         s2_copy(dz).start()
-    send_first_halves(EARLY, HEADS)
     for dz in range(1, 4):
         slot = lax.rem(z + dz, 4)
         remote(zb.at[slot], zb.at[slot], s2_s.at[dz], s2_r.at[slot], sibling).wait_recv()
@@ -176,10 +185,6 @@
         step = i + 1
         j = lax.rem(xy + PLANE - step // 2 + 8 * lax.rem(step, 2), PLANE)
         s3_copy(j).start()
-
-    for i in range(2, 4):
-        local_in[i].wait()
-        remote_in[i].wait_recv()
 
     block0 = seq - c
     row = lax.broadcasted_iota(jnp.int32, (HALF, BLOCK), 0)
@@ -198,14 +203,24 @@
     def r1_copy(j):
         return remote(fk.at[j], rin.at[xy], r1_s.at[j], r1_r.at[xy], plane_dev(j))
 
-    def pg_copy(h):
-        return remote(pk.at[h], pr.at[h], pg_s.at[h], pg_r.at[h], partner)
+    def st_copy(b):
+        return remote(st.at[b], sr.at[b], st_s.at[b], st_r.at[b], partner)
+
+    lane = lax.broadcasted_iota(jnp.int32, (BLOCK, DH), 1)
 
     @pl.loop(0, HEADS)
     def _(i):
         h = lax.rem(xy + i, HEADS)
         cols = head_cols(h)
 
+        @pl.when(i < HEADS - EARLY)
+        def _():
+            swap(i + EARLY, i + EARLY + 1, False)
+
+        @pl.when(i < HEADS - EARLY_BACK)
+        def _():
+            swap(i + EARLY_BACK, i + EARLY_BACK + 1, True)
+
         for kv in range(2):
             slot = kv * HEADS + h
 
@@ -216,7 +231,7 @@
         @pl.when(t == 1)
         def _():
             for k in range(4):
-                pv_copy(h, k).wait_recv()
+                swap_copy(h, k, False).wait_recv()
 
         q = [qb[p, :, cols] for p in range(2)]
         g = [gb[p, :, cols] for p in range(2)]
@@ -254,17 +269,20 @@
             def _():
                 r1_copy(j).start()
 
+        batch = i // 4
+        place = lax.rem(i, 4) * 4
+        stats = st[batch]
+        for k, value in enumerate((top, inv, delta)):
+            stats = jnp.where(lane == place + k, value, stats)
+        st[batch] = stats
+
+        @pl.when(jnp.logical_and(t == 1, lax.rem(i, 4) == 3))
+        def _():
+            st_copy(batch).start()
+
         for p in range(2):
-            own_k = t_dot(d_half[p], q[p]) * SCALE
-            own_v = t_dot(w_half[p], g[p])
-            pk[h, 0, p] = own_k[:HALF].astype(jnp.bfloat16)
-            pk[h, 1, p] = own_v[:HALF].astype(jnp.bfloat16)
-            okf[p, :, cols] = own_k[HALF:]
-            ovf[p, :, cols] = own_v[HALF:]
-
-        @pl.when(t == 1)
-        def _():
-            pg_copy(h).start()
+            okf[p, :, cols] = t_dot(d_half[p][:, HALF:], q[p]) * SCALE
+            ovf[p, :, cols] = t_dot(w_half[p][:, HALF:], g[p])
 
         grad_q = dot(d_far, ka) + jnp.concatenate([dot(d_half[p], keys[p]) for p in range(2)], 0)
         grad_q = (grad_q * SCALE).astype(jnp.bfloat16)
@@ -284,6 +302,38 @@
         remote_out[i].start()
         local_out[i].start()
 
+    def cross(begin, end):
+        @pl.when(t == 0)
+        def _():
+            for b in range(begin // 4, (end + 3) // 4):
+                if begin <= 4 * b:
+                    st_copy(b).wait_recv()
+
+            @pl.loop(begin, end)
+            def _(i):
+                h = lax.rem(xy + i, HEADS)
+                cols = head_cols(h)
+                for k in range(4):
+                    swap_copy(h, k, True).wait_recv()
+                stats = sr[i // 4]
+                place = lax.rem(i, 4) * 4
+                top, inv, delta = [
+                    jnp.sum(jnp.where(lane == place + k, stats, 0.0), 1, keepdims=True) for k in range(3)
+                ]
+                q = [q1b[p, :, cols] for p in range(2)]
+                g = [g1b[p, :, cols] for p in range(2)]
+                s = jnp.concatenate([dot_t(q[p], kc[p, HALF:BLOCK, cols]) for p in range(2)], 0) * SCALE
+                dp = jnp.concatenate([dot_t(g[p], vc[p, HALF:BLOCK, cols]) for p in range(2)], 0)
+                prob = jnp.exp(s - top) * inv
+                w = prob.astype(jnp.bfloat16)
+                d = (prob * (dp - delta)).astype(jnp.bfloat16)
+                for p in range(2):
+                    rows = slice(p * HALF, (p + 1) * HALF)
+                    okf[p, :, cols] += t_dot(d[rows], q[p]) * SCALE
+                    ovf[p, :, cols] += t_dot(w[rows], g[p])
+
+    cross(0, 4)
+
     @pl.loop(0, PLANE)
     def _(slot):
         @pl.when(slot != xy)
@@ -304,6 +354,7 @@
     for dz in range(1, 4):
         r2_copy(dz).start()
     zr[z] = zs[t]
+    cross(4, 6)
     for dz in range(1, 4):
         slot = lax.rem(z + dz, 4)
         remote(zs.at[0], zr.at[slot], r2_s.at[dz], r2_r.at[slot], sibling).wait_recv()
@@ -323,16 +374,7 @@
         def _():
             r3_copy(j).start()
 
-    @pl.when(t == 0)
-    def _():
-        @pl.loop(0, HEADS)
-        def _(i):
-            h = lax.rem(xy + i, HEADS)
-            pg_copy(h).wait_recv()
-            cols = head_cols(h)
-            for p in range(2):
-                okf[p, :, cols] += pr[h, 0, p].astype(jnp.float32)
-                ovf[p, :, cols] += pr[h, 1, p].astype(jnp.float32)
+    cross(6, HEADS)
 
     @pl.when(low_y)
     def _():
@@ -373,18 +415,19 @@
         def _(i):
             s1_copy(lax.rem(xy + i, PLANE)).wait_send()
 
-    @pl.when(t == 0)
-    def _():
-        @pl.loop(0, HEADS)
-        def _(h):
-            for k in range(4):
-                pv_copy(h, k).wait_send()
+    for back in (False, True):
+
+        @pl.when(t == (1 if back else 0))
+        def _():
+            @pl.loop(0, HEADS)
+            def _(h):
+                for k in range(4):
+                    swap_copy(h, k, back).wait_send()
 
     @pl.when(t == 1)
     def _():
-        @pl.loop(0, HEADS)
-        def _(h):
-            pg_copy(h).wait_send()
+        for b in range(2):
+            st_copy(b).wait_send()
 
     for dz in range(1, 4):
         s2_copy(dz).wait_send()
@@ -446,8 +489,10 @@
         pltpu.VMEM((PLANE, *half), bf16),
         pltpu.VMEM((2, HALF, WIDE), f32),
         pltpu.VMEM((2, HALF, WIDE), f32),
-        pltpu.VMEM((HEADS, 2, 2, *half), bf16),
-        pltpu.VMEM((HEADS, 2, 2, *half), bf16),
+        pltpu.VMEM((2, HALF, WIDE), bf16),
+        pltpu.VMEM((2, HALF, WIDE), bf16),
+        pltpu.VMEM((2, BLOCK, DH), f32),
+        pltpu.VMEM((2, BLOCK, DH), f32),
         pltpu.VMEM((2, HALF, WIDE), bf16),
         pltpu.VMEM((2, HALF, WIDE), bf16),
         pltpu.VMEM((2, HALF, WIDE), bf16),
@@ -460,7 +505,7 @@
         dma((PLANE,)), dma((PLANE,)),
         dma((4,)), dma((4,)),
         dma((8,)), dma((PLANE,)),
-        dma((HEADS,)), dma((HEADS,)),
+        dma((2,)), dma((2,)),
         dma((4,)), dma((4,)), dma((4,)),
     ]
     results = pl.pallas_call(

time: 76.6 us -> 71.1 us (0.928); the launches traced: 75.2 us -> 71 us
  Pallas kernels: 73.9 us -> 69.7 us
    pallas_call x1, Pallas kernels: 71.4 us -> 67.3 us  [on_device(): pl.pallas_call(kernel, out_shape=[jax.ShapeDtypeStruct(queries.shape, bf1...]
where the time goes in v2:
time: 71.1 us; the launch traced here: 71 us
  Pallas kernels  69.7 us (98%)
  between operations  1.29 us (2%)
    pallas_call x1, Pallas kernels, on_device(): pl.pallas_call(kernel, out_shape=[jax.ShapeDtypeStruct(queries.shape, bf1...  67.3 us
    pallas_call x1, Pallas kernels, on_device(): pl.pallas_call(write_out, out_shape=[jax.ShapeDtypeStruct(queries.shape,...  2.42 us

profile of v2, /device:TPU:1, one launch (start us, length us, event | category | flops | bytes accessed | tf_op | source)
XLA Modules:
  0.0 71.0 jit_solution(9763693859284757080)
XLA Ops:
  1.3 67.3 %anchor_attention.1 = (bf16[128,2048]{1,0:T(8,128)(2,1)}, bf16[128,2048]{1,0:T(8,128)(2,1)}, bf16[128,2048]{1,0:T(8,128)(2,1)}, bf16[128,2048]{1,0:T(8,128)(2,1)}) custom-call(s32[1]{0:T(128)S(6)} %copy.10.anchor, s32[64]{0:T(128)} %offsets.1, bf16[128,2048]{1,0:T(8,128)(2,1)} %q_in.1, bf16[128,2048]{1,0:T(8,128)(2,1)} %k_in.1, bf16[128,2048]{1,0:T(8,128)(2,1)} %v_in.1, ...), custom_call_target="tpu_custom_call" | custom-call | tf_op jit(solution)/shard_map/anchor_attention/pallas_call | solution.py:511
  68.6 2.4 %write_out.1 = (bf16[128,2048]{1,0:T(8,128)(2,1)}, bf16[128,2048]{1,0:T(8,128)(2,1)}, bf16[128,2048]{1,0:T(8,128)(2,1)}, bf16[128,2048]{1,0:T(8,128)(2,1)}) custom-call(bf16[128,2048]{1,0:T(8,128)(2,1)} %get-tuple-element.8.refs_0_, bf16[128,2048]{1,0:T(8,128)(2,1)} %get-tuple-element.9.refs_1_, bf16[128,2048]{1,0:T(8,128)(2,1)} %get-tuple-element.10.refs_2_, ...), custom_call_target="tpu_custom_call" | custom-call | tf_op jit(solution)/shard_map/write_out/pallas_call | solution.py:522

commit v3 on v2

--- a/solution.py
+++ b/solution.py
@@ -15,7 +15,7 @@
 MESH = pl.DeviceIdType.MESH
 LOW = -1e30
 EARLY = 3
-EARLY_BACK = 3
+AHEAD = 5
 
 
 def dot_t(a, b):
@@ -64,6 +64,12 @@
             src_ref=src, dst_ref=dst, send_sem=ss, recv_sem=rs, device_id=dev, device_id_type=MESH
         )
 
+    def sent(shape_of, sem):
+        remote(shape_of, shape_of, sem, sem, sibling).wait_send()
+
+    def landed(shape_of, sem):
+        remote(shape_of, shape_of, sem, sem, sibling).wait_recv()
+
     def head_cols(h):
         return pl.ds(pl.multiple_of(h * DH, DH), DH)
 
@@ -122,7 +128,7 @@
             )
 
     def s1_copy(j):
-        return remote(sel.at[j], cand.at[lax.rem(xy, 8)], s1_s.at[j], s1_r.at[lax.rem(xy, 8)], plane_dev(j))
+        return remote(sel.at[j], cand.at[lax.rem(xy, 8)], s1_s, s1_r, plane_dev(j))
 
     @pl.when(low_y)
     def _():
@@ -140,7 +146,7 @@
         else:
             buf, far_buf, rows, far_rows = (kc, vc)[i % 2], (kc, vc)[i % 2], own_rows, prev_rows
         return remote(
-            buf.at[p, rows, cols], far_buf.at[p, far_rows, cols], sw_s.at[h, i], sw_r.at[h, i], partner
+            buf.at[p, rows, cols], far_buf.at[p, far_rows, cols], sw_s, sw_r.at[h], partner
         )
 
     def swap(begin, end, back):
@@ -156,29 +162,29 @@
     for i in range(2, 4):
         local_in[i].wait()
         remote_in[i].wait_recv()
-    swap(0, EARLY_BACK, True)
-
-    @pl.loop(0, 8)
-    def _(slot):
-        @pl.when(slot != xy)
-        def _():
-            remote(sel.at[0], cand.at[slot], s1_s.at[0], s1_r.at[slot], sibling).wait_recv()
+    swap(0, EARLY, True)
+
+    @pl.when(low_y)
+    def _():
+        landed(cand.at[pl.ds(0, 7)], s1_r)
+
+    @pl.when(jnp.logical_not(low_y))
+    def _():
+        landed(cand, s1_r)
 
     zb[z] = cand[a_xy]
 
     def s2_copy(dz):
-        return remote(zb.at[z], zb.at[z], s2_s.at[dz], s2_r.at[z], z_dev(lax.rem(z + dz, 4)))
+        return remote(zb.at[z], zb.at[z], s2_s, s2_r, z_dev(lax.rem(z + dz, 4)))
 
     for dz in range(1, 4):
         s2_copy(dz).start()
-    for dz in range(1, 4):
-        slot = lax.rem(z + dz, 4)
-        remote(zb.at[slot], zb.at[slot], s2_s.at[dz], s2_r.at[slot], sibling).wait_recv()
+    landed(zb.at[pl.ds(0, 3)], s2_r)
     kva[xy, 0:HALF, :] = zb[a_zl]
     kva[xy, HALF:BLOCK, :] = zb[2 + a_zl]
 
     def s3_copy(j):
-        return remote(kva.at[xy], kva.at[xy], s3_s.at[j], s3_r.at[xy], plane_dev(j))
+        return remote(kva.at[xy], kva.at[xy], s3_s, s3_r.at[xy], plane_dev(j))
 
     @pl.loop(0, PLANE - 1)
     def _(i):
@@ -186,6 +192,8 @@
         j = lax.rem(xy + PLANE - step // 2 + 8 * lax.rem(step, 2), PLANE)
         s3_copy(j).start()
 
+    swap(EARLY, AHEAD, False)
+    swap(EARLY, AHEAD, True)
     block0 = seq - c
     row = lax.broadcasted_iota(jnp.int32, (HALF, BLOCK), 0)
     col = lax.broadcasted_iota(jnp.int32, (HALF, BLOCK), 1)
@@ -201,7 +209,7 @@
     )
 
     def r1_copy(j):
-        return remote(fk.at[j], rin.at[xy], r1_s.at[j], r1_r.at[xy], plane_dev(j))
+        return remote(fk.at[j], rin.at[xy], r1_s, r1_r, plane_dev(j))
 
     def st_copy(b):
         return remote(st.at[b], sr.at[b], st_s.at[b], st_r.at[b], partner)
@@ -213,25 +221,21 @@
         h = lax.rem(xy + i, HEADS)
         cols = head_cols(h)
 
-        @pl.when(i < HEADS - EARLY)
+        @pl.when(i < HEADS - AHEAD)
         def _():
-            swap(i + EARLY, i + EARLY + 1, False)
-
-        @pl.when(i < HEADS - EARLY_BACK)
-        def _():
-            swap(i + EARLY_BACK, i + EARLY_BACK + 1, True)
+            swap(i + AHEAD, i + AHEAD + 1, False)
+            swap(i + AHEAD, i + AHEAD + 1, True)
 
         for kv in range(2):
             slot = kv * HEADS + h
 
             @pl.when(slot != xy)
             def _():
-                remote(kva.at[slot], kva.at[slot], s3_s.at[0], s3_r.at[slot], sibling).wait_recv()
+                landed(kva.at[slot], s3_r.at[slot])
 
         @pl.when(t == 1)
         def _():
-            for k in range(4):
-                swap_copy(h, k, False).wait_recv()
+            landed(cand.at[pl.ds(0, 4)], sw_r.at[h])
 
         q = [qb[p, :, cols] for p in range(2)]
         g = [gb[p, :, cols] for p in range(2)]
@@ -313,8 +317,7 @@
             def _(i):
                 h = lax.rem(xy + i, HEADS)
                 cols = head_cols(h)
-                for k in range(4):
-                    swap_copy(h, k, True).wait_recv()
+                landed(cand.at[pl.ds(0, 4)], sw_r.at[h])
                 stats = sr[i // 4]
                 place = lax.rem(i, 4) * 4
                 top, inv, delta = [
@@ -332,14 +335,20 @@
                     okf[p, :, cols] += t_dot(d[rows], q[p]) * SCALE
                     ovf[p, :, cols] += t_dot(w[rows], g[p])
 
+    for copy in remote_in:
+        copy.wait_send()
+
+    @pl.when(low_y)
+    def _():
+        sent(sel.at[pl.ds(0, PLANE - 1)], s1_s)
+
+    sent(zb.at[pl.ds(0, 3)], s2_s)
+    sent(kva.at[pl.ds(0, PLANE - 1)], s3_s)
+    sent(kc, sw_s)
+
     cross(0, 4)
 
-    @pl.loop(0, PLANE)
-    def _(slot):
-        @pl.when(slot != xy)
-        def _():
-            remote(fk.at[slot], rin.at[slot], r1_s.at[0], r1_r.at[slot], sibling).wait_recv()
-
+    landed(rin.at[pl.ds(0, PLANE - 1)], r1_r)
     rin[xy] = fk[xy]
     acc = rin[0].astype(jnp.float32)
     for slot in range(1, PLANE):
@@ -349,22 +358,21 @@
 
     def r2_copy(dz):
         z_ = lax.rem(z + dz, 4)
-        return remote(zs.at[z_ // 2], zr.at[z], r2_s.at[dz], r2_r.at[z], z_dev(z_))
+        return remote(zs.at[z_ // 2], zr.at[z], r2_s, r2_r, z_dev(z_))
 
     for dz in range(1, 4):
         r2_copy(dz).start()
     zr[z] = zs[t]
     cross(4, 6)
-    for dz in range(1, 4):
-        slot = lax.rem(z + dz, 4)
-        remote(zs.at[0], zr.at[slot], r2_s.at[dz], r2_r.at[slot], sibling).wait_recv()
+    sent(fk.at[pl.ds(0, PLANE - 1)], r1_s)
+    landed(zr.at[pl.ds(0, 3)], r2_r)
     total = zr[0].astype(jnp.float32)
     for slot in range(1, 4):
         total = total + zr[slot].astype(jnp.float32)
     an[...] = total.astype(jnp.bfloat16)
 
     def r3_copy(j):
-        return remote(an, ank.at[xy], r3_s.at[j], r3_r.at[xy], plane_dev(j))
+        return remote(an, ank.at[xy], r3_s, r3_r, plane_dev(j))
 
     @pl.loop(0, 8)
     def _(i):
@@ -375,16 +383,17 @@
             r3_copy(j).start()
 
     cross(6, HEADS)
+    sent(zr.at[pl.ds(0, 3)], r2_s)
+
+    @pl.when(t == 1)
+    def _():
+        for b in range(2):
+            st_copy(b).wait_send()
 
     @pl.when(low_y)
     def _():
         ank[xy] = an[...]
-
-        @pl.loop(0, PLANE)
-        def _(slot):
-            @pl.when(slot != xy)
-            def _():
-                remote(an, ank.at[slot], r3_s.at[0], r3_r.at[slot], sibling).wait_recv()
+        landed(ank.at[pl.ds(0, PLANE - 1)], r3_r)
 
     for p in (other, c):
         for kv, (grads, out) in enumerate(((okf, gk_b), (ovf, gv_b))):
@@ -406,45 +415,13 @@
             else:
                 local_out[2 + kv].start()
 
-    for copy in remote_in:
-        copy.wait_send()
-
     @pl.when(low_y)
     def _():
-        @pl.loop(1, PLANE)
-        def _(i):
-            s1_copy(lax.rem(xy + i, PLANE)).wait_send()
-
-    for back in (False, True):
-
-        @pl.when(t == (1 if back else 0))
-        def _():
-            @pl.loop(0, HEADS)
-            def _(h):
-                for k in range(4):
-                    swap_copy(h, k, back).wait_send()
-
-    @pl.when(t == 1)
-    def _():
-        for b in range(2):
-            st_copy(b).wait_send()
-
-    for dz in range(1, 4):
-        s2_copy(dz).wait_send()
-        r2_copy(dz).wait_send()
-
-    @pl.loop(0, PLANE)
-    def _(j):
-        @pl.when(j != xy)
-        def _():
-            s3_copy(j).wait_send()
-            r1_copy(j).wait_send()
-
-    @pl.loop(0, 8)
-    def _(j):
-        @pl.when(j != xy)
-        def _():
-            r3_copy(j).wait_send()
+        sent(ank.at[pl.ds(0, 7)], r3_s)
+
+    @pl.when(jnp.logical_not(low_y))
+    def _():
+        sent(ank.at[pl.ds(0, 8)], r3_s)
 
     for copy in local_out:
         copy.wait()
@@ -498,13 +475,13 @@
         pltpu.VMEM((2, HALF, WIDE), bf16),
         pltpu.VMEM((2, HALF, WIDE), bf16),
         dma((4,)), dma((4,)), dma((4,)),
-        dma((HEADS, 4)), dma((HEADS, 4)),
-        dma((PLANE,)), dma((8,)),
-        dma((4,)), dma((4,)),
-        dma((PLANE,)), dma((PLANE,)),
-        dma((PLANE,)), dma((PLANE,)),
-        dma((4,)), dma((4,)),
-        dma((8,)), dma((PLANE,)),
+        dma, dma((HEADS,)),
+        dma, dma,
+        dma, dma,
+        dma, dma((PLANE,)),
+        dma, dma,
+        dma, dma,
+        dma, dma,
         dma((2,)), dma((2,)),
         dma((4,)), dma((4,)), dma((4,)),
     ]

time: 71.1 us -> 68.1 us (0.958)
  Pallas kernels: 69.7 us -> 66.7 us
    pallas_call x1, Pallas kernels: 67.3 us -> 64.2 us  [on_device(): pl.pallas_call(kernel, out_shape=[jax.ShapeDtypeStruct(queries.shape, bf1...]
where the time goes in v3:
time: 68.1 us; the launch traced here: 67.9 us
  Pallas kernels  66.7 us (98%)
  between operations  1.29 us (2%)
    pallas_call x1, Pallas kernels, on_device(): pl.pallas_call(kernel, out_shape=[jax.ShapeDtypeStruct(queries.shape, bf1...  64.2 us
    pallas_call x1, Pallas kernels, on_device(): pl.pallas_call(write_out, out_shape=[jax.ShapeDtypeStruct(queries.shape,...  2.42 us

profile of v3, /device:TPU:1, one launch (start us, length us, event | category | flops | bytes accessed | tf_op | source)
XLA Modules:
  0.0 67.9 jit_solution(14326012743479281164)
XLA Ops:
  1.3 64.2 %anchor_attention.1 = (bf16[128,2048]{1,0:T(8,128)(2,1)}, bf16[128,2048]{1,0:T(8,128)(2,1)}, bf16[128,2048]{1,0:T(8,128)(2,1)}, bf16[128,2048]{1,0:T(8,128)(2,1)}) custom-call(s32[1]{0:T(128)S(6)} %copy.10.anchor, s32[64]{0:T(128)} %offsets.1, bf16[128,2048]{1,0:T(8,128)(2,1)} %q_in.1, bf16[128,2048]{1,0:T(8,128)(2,1)} %k_in.1, bf16[128,2048]{1,0:T(8,128)(2,1)} %v_in.1, ...), custom_call_target="tpu_custom_call" | custom-call | tf_op jit(solution)/shard_map/anchor_attention/pallas_call | solution.py:488
  65.5 2.4 %write_out.1 = (bf16[128,2048]{1,0:T(8,128)(2,1)}, bf16[128,2048]{1,0:T(8,128)(2,1)}, bf16[128,2048]{1,0:T(8,128)(2,1)}, bf16[128,2048]{1,0:T(8,128)(2,1)}) custom-call(bf16[128,2048]{1,0:T(8,128)(2,1)} %get-tuple-element.8.refs_0_, bf16[128,2048]{1,0:T(8,128)(2,1)} %get-tuple-element.9.refs_1_, bf16[128,2048]{1,0:T(8,128)(2,1)} %get-tuple-element.10.refs_2_, ...), custom_call_target="tpu_custom_call" | custom-call | tf_op jit(solution)/shard_map/write_out/pallas_call | solution.py:499

commit v4 on v3

--- a/solution.py
+++ b/solution.py
@@ -14,7 +14,7 @@
 SCALE = DH**-0.5
 MESH = pl.DeviceIdType.MESH
 LOW = -1e30
-EARLY = 3
+EARLY = 4
 AHEAD = 5
 
 
@@ -108,7 +108,32 @@
     st[...] = jnp.zeros_like(st)
     pl.semaphore_wait(barrier, 4 + PLANE - 1)
 
-    for copy in remote_in:
+    def swap_copy(h, own, k, back, fresh):
+        cols = head_cols(h)
+        p = c if own else other
+        if back:
+            src, buf, dst, rows, far_rows = (q_in, g_in)[k], (qb, gb)[k], (q1b, g1b)[k], all_rows, all_rows
+        else:
+            src, buf, dst, rows, far_rows = (k_in, v_in)[k], (kc, vc)[k], (kc, vc)[k], own_rows, prev_rows
+        src = src.at[:, head_cols(c * HEADS + h)] if fresh else buf.at[p, rows, cols]
+        return remote(src, dst.at[p, far_rows, cols], sw_s, sw_r.at[h], partner)
+
+    def swap(begin, end, sides=(True, False), fresh=False):
+        for back in (False, True):
+
+            @pl.when(t == (1 if back else 0))
+            def _():
+                @pl.loop(begin, end)
+                def _(i):
+                    h = lax.rem(xy + i, HEADS)
+                    for own in sides:
+                        for k in range(2):
+                            swap_copy(h, own, k, back, fresh).start()
+
+    for copy in remote_in[:2]:
+        copy.start()
+    swap(0, EARLY, (True,), True)
+    for copy in remote_in[2:]:
         copy.start()
 
     a = anchor[0]
@@ -138,31 +163,10 @@
 
         cand[lax.rem(xy, 8)] = sel[xy]
 
-    def swap_copy(h, i, back):
-        p = i // 2
-        cols = head_cols(h)
-        if back:
-            buf, far_buf, rows, far_rows = (qb, gb)[i % 2], (q1b, g1b)[i % 2], all_rows, all_rows
-        else:
-            buf, far_buf, rows, far_rows = (kc, vc)[i % 2], (kc, vc)[i % 2], own_rows, prev_rows
-        return remote(
-            buf.at[p, rows, cols], far_buf.at[p, far_rows, cols], sw_s, sw_r.at[h], partner
-        )
-
-    def swap(begin, end, back):
-        @pl.when(t == (1 if back else 0))
-        def _():
-            @pl.loop(begin, end)
-            def _(i):
-                h = lax.rem(xy + i, HEADS)
-                for k in range(4):
-                    swap_copy(h, k, back).start()
-
-    swap(0, EARLY, False)
     for i in range(2, 4):
         local_in[i].wait()
         remote_in[i].wait_recv()
-    swap(0, EARLY, True)
+    swap(0, EARLY, (False,))
 
     @pl.when(low_y)
     def _():
@@ -183,17 +187,30 @@
     kva[xy, 0:HALF, :] = zb[a_zl]
     kva[xy, HALF:BLOCK, :] = zb[2 + a_zl]
 
-    def s3_copy(j):
-        return remote(kva.at[xy], kva.at[xy], s3_s, s3_r.at[xy], plane_dev(j))
-
-    @pl.loop(0, PLANE - 1)
-    def _(i):
-        step = i + 1
-        j = lax.rem(xy + PLANE - step // 2 + 8 * lax.rem(step, 2), PLANE)
-        s3_copy(j).start()
-
-    swap(EARLY, AHEAD, False)
-    swap(EARLY, AHEAD, True)
+    x, y = lax.rem(xy, 4), xy // 4
+
+    def along(slot, k, on_x, step):
+        dev = y * 4 + lax.rem(x + step, 4) if on_x else lax.rem(y + step, 4) * 4 + x
+        part = kva.at[slot, pl.ds(k * HALF, HALF), :]
+        return remote(part, part, s3_s, s3_r.at[slot, k], plane_dev(dev))
+
+    def arrived(slot, k):
+        landed(kva.at[slot, pl.ds(k * HALF, HALF), :], s3_r.at[slot, k])
+
+    for second_leg in (False, True):
+        for step in (1, 3, 2):
+            for k in range(2):
+                along(xy, k, (k == 0) != second_leg, step).start()
+
+    swap(EARLY, AHEAD)
+
+    for n in (1, 3, 2):
+        for k in range(2):
+            slot = y * 4 + lax.rem(x + n, 4) if k == 0 else lax.rem(y + n, 4) * 4 + x
+            arrived(slot, k)
+            for step in (1, 3, 2):
+                along(slot, k, k == 1, step).start()
+
     block0 = seq - c
     row = lax.broadcasted_iota(jnp.int32, (HALF, BLOCK), 0)
     col = lax.broadcasted_iota(jnp.int32, (HALF, BLOCK), 1)
@@ -223,15 +240,20 @@
 
         @pl.when(i < HEADS - AHEAD)
         def _():
-            swap(i + AHEAD, i + AHEAD + 1, False)
-            swap(i + AHEAD, i + AHEAD + 1, True)
+            swap(i + AHEAD, i + AHEAD + 1)
 
         for kv in range(2):
             slot = kv * HEADS + h
 
             @pl.when(slot != xy)
             def _():
-                landed(kva.at[slot], s3_r.at[slot])
+                @pl.when(slot // 4 != y)
+                def _():
+                    arrived(slot, 0)
+
+                @pl.when(lax.rem(slot, 4) != x)
+                def _():
+                    arrived(slot, 1)
 
         @pl.when(t == 1)
         def _():
@@ -247,25 +269,25 @@
         va = kva[HEADS + h]
         s_far = dot_t(q2, ka) * SCALE + far_bias
         s_own = jnp.concatenate([dot_t(q[p], keys[p]) for p in range(2)], 0) * SCALE + own_bias
-        top = jnp.maximum(jnp.max(s_own, 1, keepdims=True), jnp.max(s_far, 1, keepdims=True))
+        top = jnp.max(jnp.maximum(s_own, s_far), 1, keepdims=True)
         e_own = jnp.exp(s_own - top)
         e_far = jnp.exp(s_far - top)
-        total = jnp.sum(e_own, 1, keepdims=True) + jnp.sum(e_far, 1, keepdims=True)
+        total = jnp.sum(e_own + e_far, 1, keepdims=True)
         inv = 1.0 / total
-        p_own = e_own * inv
-        p_far = e_far * inv
-        w_own = p_own.astype(jnp.bfloat16)
-        w_far = p_far.astype(jnp.bfloat16)
+        w_own = e_own.astype(jnp.bfloat16)
+        w_far = e_far.astype(jnp.bfloat16)
         w_half = [w_own[p * HALF : (p + 1) * HALF] for p in range(2)]
         mixed = dot(w_far, va) + jnp.concatenate([dot(w_half[p], values[p]) for p in range(2)], 0)
+        mixed = mixed * inv
+        scaled_g = (g2.astype(jnp.float32) * inv).astype(jnp.bfloat16)
         att = mixed.astype(jnp.bfloat16)
         delta = jnp.sum(g2.astype(jnp.float32) * att.astype(jnp.float32), 1, keepdims=True)
-        d_far = (p_far * (dot_t(g2, va) - delta)).astype(jnp.bfloat16)
+        d_far = (e_far * ((dot_t(g2, va) - delta) * inv)).astype(jnp.bfloat16)
         dp_own = jnp.concatenate([dot_t(g[p], values[p]) for p in range(2)], 0)
-        d_own = (p_own * (dp_own - delta)).astype(jnp.bfloat16)
+        d_own = (e_own * ((dp_own - delta) * inv)).astype(jnp.bfloat16)
         d_half = [d_own[p * HALF : (p + 1) * HALF] for p in range(2)]
         fk[h] = (t_dot(d_far, q2) * SCALE).astype(jnp.bfloat16)
-        fk[HEADS + h] = t_dot(w_far, g2).astype(jnp.bfloat16)
+        fk[HEADS + h] = t_dot(w_far, scaled_g).astype(jnp.bfloat16)
         for kv in range(2):
             j = kv * HEADS + h
 
@@ -286,7 +308,7 @@
 
         for p in range(2):
             okf[p, :, cols] = t_dot(d_half[p][:, HALF:], q[p]) * SCALE
-            ovf[p, :, cols] = t_dot(w_half[p][:, HALF:], g[p])
+            ovf[p, :, cols] = t_dot(w_half[p][:, HALF:], scaled_g[p * HALF : (p + 1) * HALF])
 
         grad_q = dot(d_far, ka) + jnp.concatenate([dot(d_half[p], keys[p]) for p in range(2)], 0)
         grad_q = (grad_q * SCALE).astype(jnp.bfloat16)
@@ -363,7 +385,6 @@
     for dz in range(1, 4):
         r2_copy(dz).start()
     zr[z] = zs[t]
-    cross(4, 6)
     sent(fk.at[pl.ds(0, PLANE - 1)], r1_s)
     landed(zr.at[pl.ds(0, 3)], r2_r)
     total = zr[0].astype(jnp.float32)
@@ -382,7 +403,7 @@
         def _():
             r3_copy(j).start()
 
-    cross(6, HEADS)
+    cross(4, HEADS)
     sent(zr.at[pl.ds(0, 3)], r2_s)
 
     @pl.when(t == 1)
@@ -478,7 +499,7 @@
         dma, dma((HEADS,)),
         dma, dma,
         dma, dma,
-        dma, dma((PLANE,)),
+        dma, dma((PLANE, 2)),
         dma, dma,
         dma, dma,
         dma, dma,

time: 68.1 us -> 64.9 us (0.953)
  Pallas kernels: 66.7 us -> 63.5 us
    pallas_call x1, Pallas kernels: 64.2 us -> 61.1 us  [on_device(): pl.pallas_call(kernel, out_shape=[jax.ShapeDtypeStruct(queries.shape, bf1...]
where the time goes in v4:
time: 64.9 us; the launch traced here: 64.8 us
  Pallas kernels  63.5 us (98%)
  between operations  1.29 us (2%)
    pallas_call x1, Pallas kernels, on_device(): pl.pallas_call(kernel, out_shape=[jax.ShapeDtypeStruct(queries.shape, bf1...  61.1 us
    pallas_call x1, Pallas kernels, on_device(): pl.pallas_call(write_out, out_shape=[jax.ShapeDtypeStruct(queries.shape,...  2.42 us

profile of v4, /device:TPU:1, one launch (start us, length us, event | category | flops | bytes accessed | tf_op | source)
XLA Modules:
  0.0 64.8 jit_solution(8760532406523076239)
XLA Ops:
  1.3 61.1 %anchor_attention.1 = (bf16[128,2048]{1,0:T(8,128)(2,1)}, bf16[128,2048]{1,0:T(8,128)(2,1)}, bf16[128,2048]{1,0:T(8,128)(2,1)}, bf16[128,2048]{1,0:T(8,128)(2,1)}) custom-call(s32[1]{0:T(128)S(6)} %copy.10.anchor, s32[64]{0:T(128)} %offsets.1, bf16[128,2048]{1,0:T(8,128)(2,1)} %q_in.1, bf16[128,2048]{1,0:T(8,128)(2,1)} %k_in.1, bf16[128,2048]{1,0:T(8,128)(2,1)} %v_in.1, ...), custom_call_target="tpu_custom_call" | custom-call | tf_op jit(solution)/shard_map/anchor_attention/pallas_call | solution.py:509
  62.4 2.4 %write_out.1 = (bf16[128,2048]{1,0:T(8,128)(2,1)}, bf16[128,2048]{1,0:T(8,128)(2,1)}, bf16[128,2048]{1,0:T(8,128)(2,1)}, bf16[128,2048]{1,0:T(8,128)(2,1)}) custom-call(bf16[128,2048]{1,0:T(8,128)(2,1)} %get-tuple-element.8.refs_0_, bf16[128,2048]{1,0:T(8,128)(2,1)} %get-tuple-element.9.refs_1_, bf16[128,2048]{1,0:T(8,128)(2,1)} %get-tuple-element.10.refs_2_, ...), custom_call_target="tpu_custom_call" | custom-call | tf_op jit(solution)/shard_map/write_out/pallas_call | solution.py:520

commit v5 on v4

--- a/solution.py
+++ b/solution.py
@@ -15,7 +15,7 @@
 MESH = pl.DeviceIdType.MESH
 LOW = -1e30
 EARLY = 4
-AHEAD = 5
+AHEAD = 6
 
 
 def dot_t(a, b):
@@ -274,20 +274,20 @@
         e_far = jnp.exp(s_far - top)
         total = jnp.sum(e_own + e_far, 1, keepdims=True)
         inv = 1.0 / total
-        w_own = e_own.astype(jnp.bfloat16)
-        w_far = e_far.astype(jnp.bfloat16)
+        p_own = e_own * inv
+        p_far = e_far * inv
+        w_own = p_own.astype(jnp.bfloat16)
+        w_far = p_far.astype(jnp.bfloat16)
         w_half = [w_own[p * HALF : (p + 1) * HALF] for p in range(2)]
         mixed = dot(w_far, va) + jnp.concatenate([dot(w_half[p], values[p]) for p in range(2)], 0)
-        mixed = mixed * inv
-        scaled_g = (g2.astype(jnp.float32) * inv).astype(jnp.bfloat16)
         att = mixed.astype(jnp.bfloat16)
         delta = jnp.sum(g2.astype(jnp.float32) * att.astype(jnp.float32), 1, keepdims=True)
-        d_far = (e_far * ((dot_t(g2, va) - delta) * inv)).astype(jnp.bfloat16)
+        d_far = (p_far * (dot_t(g2, va) - delta)).astype(jnp.bfloat16)
         dp_own = jnp.concatenate([dot_t(g[p], values[p]) for p in range(2)], 0)
-        d_own = (e_own * ((dp_own - delta) * inv)).astype(jnp.bfloat16)
+        d_own = (p_own * (dp_own - delta)).astype(jnp.bfloat16)
         d_half = [d_own[p * HALF : (p + 1) * HALF] for p in range(2)]
         fk[h] = (t_dot(d_far, q2) * SCALE).astype(jnp.bfloat16)
-        fk[HEADS + h] = t_dot(w_far, scaled_g).astype(jnp.bfloat16)
+        fk[HEADS + h] = t_dot(w_far, g2).astype(jnp.bfloat16)
         for kv in range(2):
             j = kv * HEADS + h
 
@@ -308,7 +308,7 @@
 
         for p in range(2):
             okf[p, :, cols] = t_dot(d_half[p][:, HALF:], q[p]) * SCALE
-            ovf[p, :, cols] = t_dot(w_half[p][:, HALF:], scaled_g[p * HALF : (p + 1) * HALF])
+            ovf[p, :, cols] = t_dot(w_half[p][:, HALF:], g[p])
 
         grad_q = dot(d_far, ka) + jnp.concatenate([dot(d_half[p], keys[p]) for p in range(2)], 0)
         grad_q = (grad_q * SCALE).astype(jnp.bfloat16)
@@ -368,8 +368,6 @@
     sent(kva.at[pl.ds(0, PLANE - 1)], s3_s)
     sent(kc, sw_s)
 
-    cross(0, 4)
-
     landed(rin.at[pl.ds(0, PLANE - 1)], r1_r)
     rin[xy] = fk[xy]
     acc = rin[0].astype(jnp.float32)
@@ -385,6 +383,7 @@
     for dz in range(1, 4):
         r2_copy(dz).start()
     zr[z] = zs[t]
+    cross(0, 4)
     sent(fk.at[pl.ds(0, PLANE - 1)], r1_s)
     landed(zr.at[pl.ds(0, 3)], r2_r)
     total = zr[0].astype(jnp.float32)

time: 64.9 us -> 65.3 us (level)
  no operation moved by 1% of the time
where the time goes in v5:
time: 65.3 us; the launch traced here: 65.2 us
  Pallas kernels  63.9 us (98%)
  between operations  1.29 us (2%)
    pallas_call x1, Pallas kernels, on_device(): pl.pallas_call(kernel, out_shape=[jax.ShapeDtypeStruct(queries.shape, bf1...  61.5 us
    pallas_call x1, Pallas kernels, on_device(): pl.pallas_call(write_out, out_shape=[jax.ShapeDtypeStruct(queries.shape,...  2.42 us

profile of v5, /device:TPU:1, one launch (start us, length us, event | category | flops | bytes accessed | tf_op | source)
XLA Modules:
  0.0 65.2 jit_solution(599806507777160241)
XLA Ops:
  1.3 61.5 %anchor_attention.1 = (bf16[128,2048]{1,0:T(8,128)(2,1)}, bf16[128,2048]{1,0:T(8,128)(2,1)}, bf16[128,2048]{1,0:T(8,128)(2,1)}, bf16[128,2048]{1,0:T(8,128)(2,1)}) custom-call(s32[1]{0:T(128)S(6)} %copy.10.anchor, s32[64]{0:T(128)} %offsets.1, bf16[128,2048]{1,0:T(8,128)(2,1)} %q_in.1, bf16[128,2048]{1,0:T(8,128)(2,1)} %k_in.1, bf16[128,2048]{1,0:T(8,128)(2,1)} %v_in.1, ...), custom_call_target="tpu_custom_call" | custom-call | tf_op jit(solution)/shard_map/anchor_attention/pallas_call | solution.py:508
  62.7 2.4 %write_out.1 = (bf16[128,2048]{1,0:T(8,128)(2,1)}, bf16[128,2048]{1,0:T(8,128)(2,1)}, bf16[128,2048]{1,0:T(8,128)(2,1)}, bf16[128,2048]{1,0:T(8,128)(2,1)}) custom-call(bf16[128,2048]{1,0:T(8,128)(2,1)} %get-tuple-element.8.refs_0_, bf16[128,2048]{1,0:T(8,128)(2,1)} %get-tuple-element.9.refs_1_, bf16[128,2048]{1,0:T(8,128)(2,1)} %get-tuple-element.10.refs_2_, ...), custom_call_target="tpu_custom_call" | custom-call | tf_op jit(solution)/shard_map/write_out/pallas_call | solution.py:519

commit v6 on v4

--- a/solution.py
+++ b/solution.py
@@ -14,7 +14,8 @@
 SCALE = DH**-0.5
 MESH = pl.DeviceIdType.MESH
 LOW = -1e30
-EARLY = 4
+EARLY_OWN = 5
+EARLY = 3
 AHEAD = 5
 
 
@@ -132,7 +133,7 @@
 
     for copy in remote_in[:2]:
         copy.start()
-    swap(0, EARLY, (True,), True)
+    swap(0, EARLY_OWN, (True,), True)
     for copy in remote_in[2:]:
         copy.start()
 
@@ -202,7 +203,8 @@
             for k in range(2):
                 along(xy, k, (k == 0) != second_leg, step).start()
 
-    swap(EARLY, AHEAD)
+    swap(EARLY, AHEAD, (False,))
+    swap(EARLY_OWN, AHEAD, (True,))
 
     for n in (1, 3, 2):
         for k in range(2):
@@ -368,8 +370,6 @@
     sent(kva.at[pl.ds(0, PLANE - 1)], s3_s)
     sent(kc, sw_s)
 
-    cross(0, 4)
-
     landed(rin.at[pl.ds(0, PLANE - 1)], r1_r)
     rin[xy] = fk[xy]
     acc = rin[0].astype(jnp.float32)
@@ -385,6 +385,7 @@
     for dz in range(1, 4):
         r2_copy(dz).start()
     zr[z] = zs[t]
+    cross(0, 4)
     sent(fk.at[pl.ds(0, PLANE - 1)], r1_s)
     landed(zr.at[pl.ds(0, 3)], r2_r)
     total = zr[0].astype(jnp.float32)

time: 64.9 us -> 64.9 us (level)
  no operation moved by 1% of the time
where the time goes in v6:
time: 64.9 us; the launch traced here: 64.8 us
  Pallas kernels  63.5 us (98%)
  between operations  1.29 us (2%)
    pallas_call x1, Pallas kernels, on_device(): pl.pallas_call(kernel, out_shape=[jax.ShapeDtypeStruct(queries.shape, bf1...  61.1 us
    pallas_call x1, Pallas kernels, on_device(): pl.pallas_call(write_out, out_shape=[jax.ShapeDtypeStruct(queries.shape,...  2.42 us

profile of v6, /device:TPU:1, one launch (start us, length us, event | category | flops | bytes accessed | tf_op | source)
XLA Modules:
  0.0 64.8 jit_solution(6360207801340232725)
XLA Ops:
  1.3 61.1 %anchor_attention.1 = (bf16[128,2048]{1,0:T(8,128)(2,1)}, bf16[128,2048]{1,0:T(8,128)(2,1)}, bf16[128,2048]{1,0:T(8,128)(2,1)}, bf16[128,2048]{1,0:T(8,128)(2,1)}) custom-call(s32[1]{0:T(128)S(6)} %copy.10.anchor, s32[64]{0:T(128)} %offsets.1, bf16[128,2048]{1,0:T(8,128)(2,1)} %q_in.1, bf16[128,2048]{1,0:T(8,128)(2,1)} %k_in.1, bf16[128,2048]{1,0:T(8,128)(2,1)} %v_in.1, ...), custom_call_target="tpu_custom_call" | custom-call | tf_op jit(solution)/shard_map/anchor_attention/pallas_call | solution.py:510
  62.4 2.4 %write_out.1 = (bf16[128,2048]{1,0:T(8,128)(2,1)}, bf16[128,2048]{1,0:T(8,128)(2,1)}, bf16[128,2048]{1,0:T(8,128)(2,1)}, bf16[128,2048]{1,0:T(8,128)(2,1)}) custom-call(bf16[128,2048]{1,0:T(8,128)(2,1)} %get-tuple-element.8.refs_0_, bf16[128,2048]{1,0:T(8,128)(2,1)} %get-tuple-element.9.refs_1_, bf16[128,2048]{1,0:T(8,128)(2,1)} %get-tuple-element.10.refs_2_, ...), custom_call_target="tpu_custom_call" | custom-call | tf_op jit(solution)/shard_map/write_out/pallas_call | solution.py:521

commit v7 on v6

--- a/solution.py
+++ b/solution.py
@@ -282,6 +282,12 @@
         mixed = dot(w_far, va) + jnp.concatenate([dot(w_half[p], values[p]) for p in range(2)], 0)
         mixed = mixed * inv
         scaled_g = (g2.astype(jnp.float32) * inv).astype(jnp.bfloat16)
+        fk[HEADS + h] = t_dot(w_far, scaled_g).astype(jnp.bfloat16)
+
+        @pl.when(HEADS + h != xy)
+        def _():
+            r1_copy(HEADS + h).start()
+
         att = mixed.astype(jnp.bfloat16)
         delta = jnp.sum(g2.astype(jnp.float32) * att.astype(jnp.float32), 1, keepdims=True)
         d_far = (e_far * ((dot_t(g2, va) - delta) * inv)).astype(jnp.bfloat16)
@@ -289,13 +295,9 @@
         d_own = (e_own * ((dp_own - delta) * inv)).astype(jnp.bfloat16)
         d_half = [d_own[p * HALF : (p + 1) * HALF] for p in range(2)]
         fk[h] = (t_dot(d_far, q2) * SCALE).astype(jnp.bfloat16)
-        fk[HEADS + h] = t_dot(w_far, scaled_g).astype(jnp.bfloat16)
-        for kv in range(2):
-            j = kv * HEADS + h
-
-            @pl.when(j != xy)
-            def _():
-                r1_copy(j).start()
+        @pl.when(h != xy)
+        def _():
+            r1_copy(h).start()
 
         batch = i // 4
         place = lax.rem(i, 4) * 4

time: 64.9 us -> 64.3 us (level)
  no operation moved by 1% of the time
where the time goes in v7:
time: 64.3 us; the launch traced here: 64.1 us
  Pallas kernels  62.9 us (98%)
  between operations  1.29 us (2%)
    pallas_call x1, Pallas kernels, on_device(): pl.pallas_call(kernel, out_shape=[jax.ShapeDtypeStruct(queries.shape, bf1...  60.4 us
    pallas_call x1, Pallas kernels, on_device(): pl.pallas_call(write_out, out_shape=[jax.ShapeDtypeStruct(queries.shape,...  2.42 us

profile of v7, /device:TPU:1, one launch (start us, length us, event | category | flops | bytes accessed | tf_op | source)
XLA Modules:
  0.0 64.1 jit_solution(5410638276729933693)
XLA Ops:
  1.3 60.4 %anchor_attention.1 = (bf16[128,2048]{1,0:T(8,128)(2,1)}, bf16[128,2048]{1,0:T(8,128)(2,1)}, bf16[128,2048]{1,0:T(8,128)(2,1)}, bf16[128,2048]{1,0:T(8,128)(2,1)}) custom-call(s32[1]{0:T(128)S(6)} %copy.10.anchor, s32[64]{0:T(128)} %offsets.1, bf16[128,2048]{1,0:T(8,128)(2,1)} %q_in.1, bf16[128,2048]{1,0:T(8,128)(2,1)} %k_in.1, bf16[128,2048]{1,0:T(8,128)(2,1)} %v_in.1, ...), custom_call_target="tpu_custom_call" | custom-call | tf_op jit(solution)/shard_map/anchor_attention/pallas_call | solution.py:512
  61.7 2.4 %write_out.1 = (bf16[128,2048]{1,0:T(8,128)(2,1)}, bf16[128,2048]{1,0:T(8,128)(2,1)}, bf16[128,2048]{1,0:T(8,128)(2,1)}, bf16[128,2048]{1,0:T(8,128)(2,1)}) custom-call(bf16[128,2048]{1,0:T(8,128)(2,1)} %get-tuple-element.8.refs_0_, bf16[128,2048]{1,0:T(8,128)(2,1)} %get-tuple-element.9.refs_1_, bf16[128,2048]{1,0:T(8,128)(2,1)} %get-tuple-element.10.refs_2_, ...), custom_call_target="tpu_custom_call" | custom-call | tf_op jit(solution)/shard_map/write_out/pallas_call | solution.py:523
